TPU v7x, 128 devices: a whole 4x4x4 slice. The times are simulated.
128 devices in a mesh: brow: 8 (over x, core), bcol: 16 (over z, y).
Axes of the slice: x: 4, y: 4, z: 4, core: 2. Of those that a mesh axis runs over, the one named last changes fastest.
Arguments:
- fields: bfloat16 [8, 64, 640, 512], P('brow', 'bcol'), may hold values from -6 to 6
- skeleton_index: int32 [8, 64, 384], P('brow', 'bcol'), may hold values from 0 to 639, as said below
- redundant_index: int32 [8, 64, 256], P('brow', 'bcol'), may hold values from 0 to 639, as said below
- neighbours: int32 [8, 64, 6], P('brow', 'bcol'), may hold values from 0 to 8, as said below
- coupling: bfloat16 [8, 64, 2, 256, 6, 384], P('brow', 'bcol'), may hold values from -0.09375 to 0.09375
- back_coupling: bfloat16 [8, 64, 2, 384, 6, 256], P('brow', 'bcol'), may hold values from -0.109375 to 0.109375
- inverse: bfloat16 [8, 64, 2, 256, 256], P('brow', 'bcol'), may hold values from -0.25 to 0.25
Outputs:
- updated: bfloat16 [8, 64, 640, 512], P('brow', 'bcol')
Inputs may be any that keep to these rules, and one draw needn't show every extreme that they name: For each box, skeleton_index and redundant_index together name each of its 640 unknowns exactly once. For each box, skeleton_index and redundant_index together name each of its 640 unknowns exactly once. `neighbours`: each box names 6 different positions of its 3 by 3 window of boxes, never the centre 4.
All inputs are finite; a program needn't handle non-finite values.
Results may differ from a plain program's by a relative error of at most 0.0051.
Values may be sent and summed in bfloat16 or wider, within the bound.
A program may use at most 128 MiB of HBM per device.

v0:
```python
import jax
import jax.numpy as jnp
from jax import lax
from jax.sharding import PartitionSpec as P


def padded_2(block, sides, width, periodic):
    for axis, dim in sides:
        count = lax.axis_size(axis)
        forward = [(i, i + 1) for i in range(count - 1)]
        if periodic:
            forward.append((count - 1, 0))
        backward = [(target, source) for source, target in forward]
        low = lax.ppermute(
            lax.slice_in_dim(block, block.shape[dim] - width, None, axis=dim), axis, forward
        )
        high = lax.ppermute(lax.slice_in_dim(block, 0, width, axis=dim), axis, backward)
        block = jnp.concatenate([low, block, high], axis=dim)
    return block


def for_sending(value):
    return jax.tree.map(lambda a: a.astype(jnp.bfloat16) if a.dtype == jnp.float32 else a, value)


def to_complex(product, rows, half):
    real_part = product[:rows, :half] - product[rows:, half:]
    imag_part = product[:rows, half:] + product[rows:, :half]
    return jnp.concatenate([real_part, imag_part], axis=1)


def near_window(padded, box, codes, cols_box):
    row_pos = box // cols_box
    col_pos = box % cols_box
    width = padded.shape[2]
    columns = padded.shape[3]
    zero = jnp.zeros((), jnp.int32)
    pieces = []
    for slot in range(codes.shape[0]):
        code = codes[slot]
        piece = lax.dynamic_slice(
            padded, (row_pos + code // 3, col_pos + code % 3, zero, zero), (1, 1, width, columns)
        )
        pieces.append(piece.reshape(width, columns))
    return jnp.concatenate(pieces, axis=0)


def spread_skeleton(values):
    partial_pad = padded_2(values, (("brow", 0),), 1, False)
    return padded_2(partial_pad, (("bcol", 1),), 1, True)


def spread_solved(values):
    partial_pad = padded_2(for_sending(values), (("brow", 0),), 1, False).astype(values.dtype)
    return padded_2(for_sending(partial_pad), (("bcol", 1),), 1, True).astype(partial_pad.dtype)


def on_device(
    fields, skeleton_index, redundant_index, neighbours, coupling, back_coupling, inverse
):
    rows_box, cols_box, unknowns, columns = fields.shape
    skel_count = skeleton_index.shape[2]
    red_count = redundant_index.shape[2]
    nearby = neighbours.shape[2]
    half = columns // 2
    boxes = rows_box * cols_box
    skel_vals_all = jnp.take_along_axis(fields, skeleton_index[..., None], axis=2)
    red_vals_all = jnp.take_along_axis(fields, redundant_index[..., None], axis=2)
    padded = spread_skeleton(skel_vals_all)
    skel_flat = skel_vals_all.reshape(boxes, skel_count, columns)
    red_flat = red_vals_all.reshape(boxes, red_count, columns)
    box_ids = jnp.arange(boxes, dtype=jnp.int32)
    codes = neighbours.reshape(boxes, nearby)
    c_flat = coupling.reshape(boxes, 2 * red_count, nearby * skel_count)
    i_flat = inverse.reshape(boxes, 2 * red_count, red_count)

    def first(item):
        box, code, block, inv_block, red_vals = item
        window = near_window(padded, box, code, cols_box)
        product = jnp.dot(block, window, preferred_element_type=jnp.float32)
        target = red_vals.astype(jnp.float32) - to_complex(product, red_count, half)
        target_b = target.astype(jnp.bfloat16)
        solved_full = jnp.dot(inv_block, target_b, preferred_element_type=jnp.float32)
        return to_complex(solved_full, red_count, half).astype(jnp.bfloat16)

    solved = lax.map(first, (box_ids, codes, c_flat, i_flat, red_flat))
    solved_pad = spread_solved(solved.reshape(rows_box, cols_box, red_count, columns))
    b_flat = back_coupling.reshape(boxes, 2 * skel_count, nearby * red_count)

    def second(item):
        box, code, block, skel_vals = item
        window = near_window(solved_pad, box, code, cols_box)
        back_prod = jnp.dot(block, window, preferred_element_type=jnp.float32)
        renewed = skel_vals.astype(jnp.float32) - to_complex(back_prod, skel_count, half)
        return renewed.astype(jnp.bfloat16)

    renewed = lax.map(second, (box_ids, codes, b_flat, skel_flat))
    stacked = jnp.concatenate([renewed, solved], axis=1)
    order_all = jnp.concatenate(
        [skeleton_index.reshape(boxes, skel_count), redundant_index.reshape(boxes, red_count)],
        axis=1,
    )
    positions = jnp.broadcast_to(jnp.arange(unknowns, dtype=jnp.int32)[None, :], (boxes, unknowns))
    invert = jax.vmap(lambda where, values: jnp.zeros((unknowns,), jnp.int32).at[where].set(values))
    inverse_order = invert(order_all, positions)
    result = jnp.take_along_axis(stacked, inverse_order[..., None], axis=1)
    return result.reshape(rows_box, cols_box, unknowns, columns)


def solution(mesh):
    in_specs = (
        P("brow", "bcol", None, None),
        P("brow", "bcol", None),
        P("brow", "bcol", None),
        P("brow", "bcol", None),
        P("brow", "bcol", None, None, None, None),
        P("brow", "bcol", None, None, None, None),
        P("brow", "bcol", None, None, None),
    )
    out_specs = P("brow", "bcol", None, None)
    return jax.shard_map(
        on_device, mesh=mesh, in_specs=in_specs, out_specs=out_specs, check_vma=False
    )
```

profile of v0, /device:TPU:3, one launch (start us, length us, event | category | flops | bytes accessed | tf_op | source)
XLA Modules:
  0.0 445.4 jit_solution(16331617379253411225)
XLA Ops:
  1.8 18.1 %gather_fusion = bf16[1536,512]{1,0:T(8,128)(2,1)} fusion(bf16[4,640,512]{2,1,0:T(8,128)(2,1)S(1)} %bitcast.236, s32[1536]{0:T(1024)S(1)} %reshape.529), kind=kCustom, calls=%fused_computation | custom fusion | bytes 3158016 | tf_op jit(solution)/shard_map/jit(take_along_axis)/gather | solution.py:67
  21.5 2.7 collective-permute-start.1
  24.3 3.0 collective-permute-start
  27.3 16.5 %collective-permute-done.1 = bf16[1,4,384,512]{3,2,1,0:T(8,128)(2,1)S(1)} collective-permute-done((bf16[1,4,384,512]{3,2,1,0:T(8,128)(2,1)S(1)}, bf16[1,4,384,512]{3,2,1,0:T(8,128)(2,1)S(1)}, u32[]{:S(2)}, u32[]{:S(2)}) %collective-permute-start.1) | collective-permute-done | bytes 1572896 | tf_op jit(solution)/shard_map/ppermute | solution.py:17
  44.6 1.8 pad_maximum_fusion.6
  46.6 6.2 %collective-permute-start.3 = (bf16[3,1,384,512]{3,2,1,0:T(8,128)(2,1)}, bf16[3,1,384,512]{3,2,1,0:T(8,128)(2,1)}, u32[]{:S(2)}, u32[]{:S(2)}) collective-permute-start(bf16[3,1,384,512]{3,2,1,0:T(8,128)(2,1)} %get-tuple-element.349), channel_id=1, source_target_pairs={{1,0},{2,1},{3,2},{4,3},{5,4},{6,5},{7,6},{8,7},{9,8},{10,9},{11,1... | collective-permute-start | bytes 3538952 | tf_op jit(solution)/shard_map/ppermute | solution.py:17
  52.9 12.2 %gather_fusion.1 = bf16[1024,512]{1,0:T(8,128)(2,1)} fusion(bf16[4,640,512]{2,1,0:T(8,128)(2,1)S(1)} %bitcast.237, s32[1024]{0:T(1024)S(1)} %bitcast.238), kind=kCustom, calls=%fused_computation.1 | custom fusion | bytes 2105344 | tf_op jit(solution)/shard_map/jit(take_along_axis)/gather | solution.py:68
  66.6 12.8 %copy.25 = bf16[1,4,2,256,6,384]{5,4,3,2,1,0:T(8,128)(2,1)} copy(bf16[1,4,2,256,6,384]{5,3,4,2,1,0:T(8,128)(2,1)} %param.15) | data formatting | bytes 18874368 | tf_op jit(solution)/shard_map/while | solution.py:86
  79.4 19.6 %reshape.566 = bf16[4,512,2304]{2,1,0:T(8,128)(2,1)} reshape(bf16[1,4,2,256,6,384]{5,4,3,2,1,0:T(8,128)(2,1)} %copy.25) | data formatting | bytes 18874368 | tf_op jit(solution)/shard_map/while | solution.py:86
  100.8 5.7 %pad_maximum_fusion.1 = bf16[3,6,384,512]{3,2,1,0:T(8,128)(2,1)} fusion(bf16[3,1,384,512]{3,2,1,0:T(8,128)(2,1)} %collective-permute-done.3, bf16[1,4,384,512]{3,2,1,0:T(8,128)(2,1)S(1)} %copy-done.8, bf16[1,4,384,512]{3,2,1,0:T(8,128)(2,1)S(1)} %copy-done.3, bf16[1,4,384,512]{3,2,1,0:T(8,128)(2,1)} %copy-done.9, ...), kind=kLoop, calls=%fused_computation.54 | loop fusion | flops 14155776 | bytes 14155776 | tf_op jit(solution)/shard_map/concatenate | solution.py:18
  106.6 124.9 %while.26 = (s32[]{:T(128)}, bf16[4,256,512]{2,1,0:T(8,128)(2,1)S(1)}, bf16[4,512,256]{2,1,0:T(8,128)(2,1)}, bf16[4,256,512]{1,2,0:T(8,128)(2,1)}, bf16[4,512,23...) while((s32[]{:T(128)}, ...), condition=%wide.region_2.3_spmd, body=%wide.region_1.2_spmd.sunk | while | flops 1343619200 | bytes 17042144 | solution.py:86
  116.1 1.8 bitcast_dynamic-update-slice_fusion.25
  119.6 1.8 bitcast_dynamic-update-slice_fusion.26
  123.3 1.8 bitcast_dynamic-update-slice_fusion.27
  126.8 1.8 bitcast_dynamic-update-slice_fusion.28
  130.5 1.8 bitcast_dynamic-update-slice_fusion.29
  132.3 3.8 fusion.59
  147.3 1.8 bitcast_dynamic-update-slice_fusion.25
  150.8 1.8 bitcast_dynamic-update-slice_fusion.26
  154.5 1.8 bitcast_dynamic-update-slice_fusion.27
  158.0 1.8 bitcast_dynamic-update-slice_fusion.28
  161.7 1.8 bitcast_dynamic-update-slice_fusion.29
  163.5 3.8 fusion.59
  178.5 1.8 bitcast_dynamic-update-slice_fusion.25
  182.1 1.8 bitcast_dynamic-update-slice_fusion.26
  185.7 1.8 bitcast_dynamic-update-slice_fusion.27
  189.2 1.8 bitcast_dynamic-update-slice_fusion.28
  192.9 1.8 bitcast_dynamic-update-slice_fusion.29
  194.7 3.8 fusion.59
  217.0 1.8 bitcast_dynamic-update-slice_fusion.27
  220.5 1.8 bitcast_dynamic-update-slice_fusion.28
  225.9 3.8 fusion.59
  231.5 3.5 collective-permute-start.5
  234.9 3.0 collective-permute-start.4
  238.2 10.6 %collective-permute-done.5 = bf16[1,4,256,512]{3,2,1,0:T(8,128)(2,1)S(1)} collective-permute-done((bf16[1,4,256,512]{3,2,1,0:T(8,128)(2,1)S(1)}, bf16[1,4,256,512]{3,2,1,0:T(8,128)(2,1)S(1)}, u32[]{:S(2)}, u32[]{:S(2)}) %collective-permute-start.5) | collective-permute-done | bytes 1048608 | tf_op jit(solution)/shard_map/ppermute | solution.py:17
  251.2 5.1 %collective-permute-start.7 = (bf16[3,1,256,512]{3,2,1,0:T(8,128)(2,1)}, bf16[3,1,256,512]{3,2,1,0:T(8,128)(2,1)S(1)}, u32[]{:S(2)}, u32[]{:S(2)}) collective-permute-start(bf16[3,1,256,512]{3,2,1,0:T(8,128)(2,1)} %get-tuple-element.351), channel_id=1, source_target_pairs={{1,0},{2,1},{3,2},{4,3},{5,4},{6,5},{7,6},{8,7},{9,8},{10,9},{11,1... | collective-permute-start | bytes 2359304 | tf_op jit(solution)/shard_map/ppermute | solution.py:17
  257.9 12.3 %copy.24 = bf16[1,4,2,384,6,256]{5,4,3,2,1,0:T(8,128)(2,1)} copy(bf16[1,4,2,384,6,256]{5,3,4,2,1,0:T(8,128)(2,1)} %param.16) | data formatting | bytes 18874368 | tf_op jit(solution)/shard_map/while | solution.py:97
  270.2 19.9 %reshape.565 = bf16[4,768,1536]{2,1,0:T(8,128)(2,1)} reshape(bf16[1,4,2,384,6,256]{5,4,3,2,1,0:T(8,128)(2,1)} %copy.24) | data formatting | bytes 18874368 | tf_op jit(solution)/shard_map/while | solution.py:97
  290.1 9.9 %scatter_custom_fusion = s32[2560]{0:T(1024)S(1)} fusion(s32[2560]{0:T(1024)S(1)} %reshape.549, s32[2560]{0:T(1024)S(1)} %reshape.551, s32[]{:T(128)} %constant.294.clone.1), kind=kCustom, calls=%fused_computation.81 | custom fusion | bytes 10244
  302.2 3.5 pad_maximum_fusion.2
  305.7 104.6 %while.27 = (s32[]{:T(128)}, bf16[4,384,512]{2,1,0:T(8,128)(2,1)}, bf16[4,384,512]{1,2,0:T(8,128)(2,1)}, bf16[4,768,1536]{2,1,0:T(8,128)(2,1)}, s32[4]{0:T(128)S...) while((s32[]{:T(128)}, bf16[4,384,512]{2,1,0:T(8,128)(2,1)}, ...), condition=%wide.region_4.5_spmd, body=%wide.region_3.4_spmd.sunk | while | flops 1208942720 | bytes 14157534 | solution.py:97
  326.6 3.1 fusion.66
  352.8 3.1 fusion.66
  378.9 3.1 fusion.66
  405.1 3.1 fusion.66
  410.3 1.9 pad_maximum_fusion.3
  412.2 29.9 %gather_fusion.2 = bf16[2560,512]{1,0:T(8,128)(2,1)} fusion(bf16[4,640,512]{2,1,0:T(8,128)(2,1)S(1)} %pad_maximum_fusion.3, s32[2560]{0:T(1024)S(1)} %reshape.543), kind=kCustom, calls=%fused_computation.2 | custom fusion | bytes 5263360 | tf_op jit(solution)/shard_map/jit(take_along_axis)/gather | solution.py:106
  442.2 3.3 broadcast_select_fusion
  (171 shorter events, 75.2 us)
Async XLA Ops:
  0.0 1.8 copy-start
  21.5 24.9 %copy-start.2 = (bf16[1,4,384,512]{3,2,1,0:T(8,128)(2,1)}, bf16[1,4,384,512]{3,2,1,0:T(8,128)(2,1)S(1)}, u32[]{:S(2)}) copy-start(bf16[1,4,384,512]{3,2,1,0:T(8,128)(2,1)S(1)} %broadcast_select_fusion.1) | copy-start | bytes 4718596
  21.5 31.3 %copy-start.16 = (s32[1,4,256]{2,1,0:T(4,128)S(1)}, s32[1,4,256]{2,1,0:T(4,128)}, u32[]{:S(2)}) copy-start(s32[1,4,256]{2,1,0:T(4,128)} %param.13) | copy-start | bytes 12292
  21.5 22.2 %collective-permute-start.1 = (bf16[1,4,384,512]{3,2,1,0:T(8,128)(2,1)S(1)}, bf16[1,4,384,512]{3,2,1,0:T(8,128)(2,1)S(1)}, u32[]{:S(2)}, u32[]{:S(2)}) collective-permute-start(bf16[1,4,384,512]{3,2,1,0:T(8,128)(2,1)S(1)} %broadcast_select_fusion.1), channel_id=1, source_target_pairs={{16,0},{32,16},{48,32},{64,48},{80,64},{96,80},{112,96},{17,1},{33... | collective-permute-start | bytes 4718600 | tf_op jit(solution)/shard_map/ppermute | solution.py:17
  24.3 20.4 %collective-permute-start = (bf16[1,4,384,512]{3,2,1,0:T(8,128)(2,1)S(1)}, bf16[1,4,384,512]{3,2,1,0:T(8,128)(2,1)S(1)}, u32[]{:S(2)}, u32[]{:S(2)}) collective-permute-start(bf16[1,4,384,512]{3,2,1,0:T(8,128)(2,1)S(1)} %broadcast_select_fusion.1), channel_id=1, source_target_pairs={{0,16},{16,32},{32,48},{48,64},{64,80},{80,96},{96,112},{1,17},{17... | collective-permute-start | bytes 4718600 | tf_op jit(solution)/shard_map/ppermute | solution.py:14
  43.7 2.7 copy-start.7
  44.6 2.0 copy-start.9
  46.6 53.5 %collective-permute-start.3 = (bf16[3,1,384,512]{3,2,1,0:T(8,128)(2,1)}, bf16[3,1,384,512]{3,2,1,0:T(8,128)(2,1)}, u32[]{:S(2)}, u32[]{:S(2)}) collective-permute-start(bf16[3,1,384,512]{3,2,1,0:T(8,128)(2,1)} %get-tuple-element.349), channel_id=1, source_target_pairs={{1,0},{2,1},{3,2},{4,3},{5,4},{6,5},{7,6},{8,7},{9,8},{10,9},{11,1... | collective-permute-start | bytes 3538952 | tf_op jit(solution)/shard_map/ppermute | solution.py:17
  52.8 47.3 %collective-permute-start.2 = (bf16[3,1,384,512]{3,2,1,0:T(8,128)(2,1)}, bf16[3,1,384,512]{3,2,1,0:T(8,128)(2,1)}, u32[]{:S(2)}, u32[]{:S(2)}) collective-permute-start(bf16[3,1,384,512]{3,2,1,0:T(8,128)(2,1)} %get-tuple-element.348), channel_id=1, source_target_pairs={{0,1},{1,2},{2,3},{3,4},{4,5},{5,6},{6,7},{7,8},{8,9},{9,10},{10,1... | collective-permute-start | bytes 3538952 | tf_op jit(solution)/shard_map/ppermute | solution.py:14
  79.4 20.8 %copy-start.8 = (bf16[1,4,384,512]{3,2,1,0:T(8,128)(2,1)S(1)}, bf16[1,4,384,512]{3,2,1,0:T(8,128)(2,1)}, u32[]{:S(2)}) copy-start(bf16[1,4,384,512]{3,2,1,0:T(8,128)(2,1)} %copy-done.7) | copy-start | bytes 4718596
  99.0 1.8 copy-start.3
  100.1 6.4 %copy-start.5 = (bf16[4,256,512]{2,1,0:T(8,128)(2,1)S(1)}, bf16[4,256,512]{2,1,0:T(8,128)(2,1)}, u32[]{:S(2)}) copy-start(bf16[4,256,512]{2,1,0:T(8,128)(2,1)} %custom-call.8) | copy-start | bytes 3145732
  100.1 6.4 %copy-start.19 = (s32[1,4,6]{2,1,0:T(4,128)S(1)}, s32[1,4,6]{2,1,0:T(4,128)}, u32[]{:S(2)}) copy-start(s32[1,4,6]{2,1,0:T(4,128)} %param.14) | copy-start | bytes 292
  106.5 131.5 %copy-start.15 = (s32[1,4,384]{2,1,0:T(4,128)S(1)}, s32[1,4,384]{2,1,0:T(4,128)}, u32[]{:S(2)}) copy-start(s32[1,4,384]{2,1,0:T(4,128)} %param.12) | copy-start | bytes 18436
  106.5 131.5 %copy-start.17 = (s32[2]{0:T(128)S(1)}, s32[2]{0:T(128)}, u32[]{:S(2)}) copy-start(s32[2]{0:T(128)} %constant.306) | copy-start | bytes 28
  106.5 131.6 %copy-start.18 = (s32[2]{0:T(128)S(1)}, s32[2]{0:T(128)}, u32[]{:S(2)}) copy-start(s32[2]{0:T(128)} %constant.309) | copy-start | bytes 28
  231.5 70.1 %copy-start.6 = (bf16[4,256,512]{2,1,0:T(8,128)(2,1)}, bf16[4,256,512]{2,1,0:T(8,128)(2,1)S(1)}, u32[]{:S(2)}) copy-start(bf16[4,256,512]{2,1,0:T(8,128)(2,1)S(1)} %get-tuple-element.283) | copy-start | bytes 3145732
  231.5 17.3 %collective-permute-start.5 = (bf16[1,4,256,512]{3,2,1,0:T(8,128)(2,1)S(1)}, bf16[1,4,256,512]{3,2,1,0:T(8,128)(2,1)S(1)}, u32[]{:S(2)}, u32[]{:S(2)}) collective-permute-start(bf16[1,4,256,512]{3,2,1,0:T(8,128)(2,1)S(1)} %bitcast.242), channel_id=1, source_target_pairs={{16,0},{32,16},{48,32},{64,48},{80,64},{96,80},{112,96},{17,1},{33... | collective-permute-start | bytes 3145736 | tf_op jit(solution)/shard_map/ppermute | solution.py:17
  234.9 14.7 %collective-permute-start.4 = (bf16[1,4,256,512]{3,2,1,0:T(8,128)(2,1)S(1)}, bf16[1,4,256,512]{3,2,1,0:T(8,128)(2,1)S(1)}, u32[]{:S(2)}, u32[]{:S(2)}) collective-permute-start(bf16[1,4,256,512]{3,2,1,0:T(8,128)(2,1)S(1)} %bitcast.243), channel_id=1, source_target_pairs={{0,16},{16,32},{32,48},{48,64},{64,80},{80,96},{96,112},{1,17},{17... | collective-permute-start | bytes 3145736 | tf_op jit(solution)/shard_map/ppermute | solution.py:14
  238.2 18.1 %copy-start.4 = (bf16[1536,512]{1,0:T(8,128)(2,1)S(1)}, bf16[1536,512]{1,0:T(8,128)(2,1)}, u32[]{:S(2)}) copy-start(bf16[1536,512]{1,0:T(8,128)(2,1)} %gather_fusion) | copy-start | bytes 4718596
  248.8 2.4 copy-start.11
  249.7 1.5 copy-start.13
  251.2 50.4 %collective-permute-start.7 = (bf16[3,1,256,512]{3,2,1,0:T(8,128)(2,1)}, bf16[3,1,256,512]{3,2,1,0:T(8,128)(2,1)S(1)}, u32[]{:S(2)}, u32[]{:S(2)}) collective-permute-start(bf16[3,1,256,512]{3,2,1,0:T(8,128)(2,1)} %get-tuple-element.351), channel_id=1, source_target_pairs={{1,0},{2,1},{3,2},{4,3},{5,4},{6,5},{7,6},{8,7},{9,8},{10,9},{11,1... | collective-permute-start | bytes 2359304 | tf_op jit(solution)/shard_map/ppermute | solution.py:17
  256.2 45.3 %collective-permute-start.6 = (bf16[3,1,256,512]{3,2,1,0:T(8,128)(2,1)}, bf16[3,1,256,512]{3,2,1,0:T(8,128)(2,1)}, u32[]{:S(2)}, u32[]{:S(2)}) collective-permute-start(bf16[3,1,256,512]{3,2,1,0:T(8,128)(2,1)} %get-tuple-element.350), channel_id=1, source_target_pairs={{0,1},{1,2},{2,3},{3,4},{4,5},{5,6},{6,7},{7,8},{8,9},{9,10},{10,1... | collective-permute-start | bytes 2359304 | tf_op jit(solution)/shard_map/ppermute | solution.py:14
  270.2 29.9 %copy-start.10 = (bf16[4,384,512]{1,2,0:T(8,128)(2,1)S(1)}, bf16[4,384,512]{1,2,0:T(8,128)(2,1)}, u32[]{:S(2)}) copy-start(bf16[4,384,512]{1,2,0:T(8,128)(2,1)} %copy.15) | copy-start | bytes 4718596
  300.1 1.5 copy-start.12
  300.1 2.1 copy-start.14
  442.2 3.3 copy-start.1
where the time goes:
time: 452 us; the launch traced here: 445 us
  local copies, waits for them, and re-layouts  220 us (49%)
  loops' own time  111 us (25%)
  matrix products  33.1 us (7%)
  other arithmetic  28.8 us (6%)
  waiting for transfers between devices  28.8 us (6%)
  starting transfers between devices  23.5 us (5%)
    another operation x1, loops' own time, on_device(): solved = lax.map(first, (box_ids, codes, c_flat, i_flat, red_flat))  55.4 us
    another operation x1, loops' own time, on_device(): renewed = lax.map(second, (box_ids, codes, b_flat, skel_flat))  55.1 us
    while x40, local copies, waits for them, and re-layouts  55 us
    while x2, local copies, waits for them, and re-layouts, on_device(): solved = lax.map(first, (box_ids, codes, c_flat, i_flat, red_flat))  32.4 us
    while x2, local copies, waits for them, and re-layouts, on_device(): renewed = lax.map(second, (box_ids, codes, b_flat, skel_flat))  32.2 us
    gather x2, local copies, waits for them, and re-layouts, on_device(): result = jnp.take_along_axis(stacked, inverse_order[..., None], axis=1)  29.9 us
    ppermute x4, waiting for transfers between devices, padded_2(): lax.ppermute(lax.slice_in_dim(block, 0, width, axis=dim), axis, backward)  27.1 us
    gather x3, local copies, waits for them, and re-layouts, on_device(): jnp.take_along_axis(fields, skeleton_index[..., None], axis=2)  19.7 us
  transfers between devices with their start and end apart: 8, of which 4 were waited for; matrix products, arithmetic and copies ran while one was open for 21% of the time, Pallas kernels for 0%

commit v1 on v0

v1 whole, which is shorter than its diff:
```python
import functools

import jax
import jax.numpy as jnp
from jax import lax
from jax.experimental import pallas as pl
from jax.experimental.pallas import tpu as pltpu
from jax.sharding import PartitionSpec as P

MESH = pl.DeviceIdType.MESH
LANES = 128
OWN, SIB, FAR = 0, 1, 2


def to_complex(product, rows, half):
    real_part = product[:rows, :half] - product[rows:, half:]
    imag_part = product[:rows, half:] + product[rows:, :half]
    return jnp.concatenate([real_part, imag_part], axis=1)


def kernel(
    sizes,
    fields_hbm, skel_idx, red_idx, near, coupling_hbm, back_hbm, inverse_hbm,
    out_hbm,
    fields, coupling, back, inverse, redundant_0, redundant_1,
    skel_0, skel_1, solved_0, solved_1, result,
    load_sem, field_sem, out_sem,
    x_send, x_recv, y_send, y_recv, s_send, s_recv, c_send, c_recv, f_send, f_recv,
):
    rows_mesh, cols_mesh, boxes, K, R, nearby = sizes
    M = K + R
    wide = boxes + 2
    half = LANES
    skel, solved, redundant = (skel_0, skel_1), (solved_0, solved_1), (redundant_0, redundant_1)

    row, col = lax.axis_index("brow"), lax.axis_index("bcol")
    core = lax.rem(row, 2)
    sibling = row + 1 - 2 * core
    across = row - 1 + 2 * core
    has_far = jnp.logical_and(across >= 0, across < rows_mesh)
    up, down = lax.rem(col + 1, cols_mesh), lax.rem(col + cols_mesh - 1, cols_mesh)
    at_sibling, at_far, at_up, at_down = (sibling, col), (across, col), (row, up), (row, down)

    barrier = pltpu.get_barrier_semaphore()
    for device in (at_sibling, at_up, at_down):
        pl.semaphore_signal(barrier, inc=1, device_id=device, device_id_type=MESH)

    @pl.when(has_far)
    def _():
        pl.semaphore_signal(barrier, inc=1, device_id=at_far, device_id_type=MESH)

    def load_fields(b):
        return pltpu.make_async_copy(fields_hbm.at[b], fields.at[b], field_sem.at[b])

    for b in range(boxes):
        load_fields(b).start()
    load_inverse = pltpu.make_async_copy(inverse_hbm, inverse, load_sem.at[0])
    load_coupling = pltpu.make_async_copy(coupling_hbm, coupling, load_sem.at[1])
    load_back = pltpu.make_async_copy(back_hbm, back, load_sem.at[2])
    load_inverse.start()
    load_coupling.start()
    load_back.start()

    def remote(window, source, target, device, send, recv):
        return pltpu.make_async_remote_copy(
            src_ref=window.at[source], dst_ref=window.at[target], send_sem=send, recv_sem=recv,
            device_id=device, device_id_type=MESH,
        )

    def x_copy(window, s, b):
        return remote(window, OWN * wide + 1 + b, FAR * wide + 1 + b, at_far, x_send.at[s, b], x_recv.at[s, b])

    def y_up(window, s):
        return remote(window, OWN * wide + boxes, OWN * wide, at_up, y_send.at[s, 0], y_recv.at[s, 0])

    def y_down(window, s):
        return remote(window, OWN * wide + 1, OWN * wide + boxes + 1, at_down, y_send.at[s, 1], y_recv.at[s, 1])

    def s_copy(window, s, b):
        return remote(window, OWN * wide + 1 + b, SIB * wide + 1 + b, at_sibling, s_send.at[s, b], s_recv.at[s, b])

    def c_up(window, s):
        return remote(window, FAR * wide + boxes, FAR * wide, at_up, c_send.at[s, 0], c_recv.at[s, 0])

    def c_down(window, s):
        return remote(window, FAR * wide + 1, FAR * wide + boxes + 1, at_down, c_send.at[s, 1], c_recv.at[s, 1])

    def f_low(window, s):
        return remote(window, OWN * wide, SIB * wide, at_sibling, f_send.at[s, 0], f_recv.at[s, 0])

    def f_high(window, s):
        return remote(window, OWN * wide + boxes + 1, SIB * wide + boxes + 1, at_sibling, f_send.at[s, 1], f_recv.at[s, 1])

    def forward_corners(window, s):
        @pl.when(has_far)
        def _():
            x_copy(window, s, 0).wait_recv()
            c_down(window, s).start()
            x_copy(window, s, boxes - 1).wait_recv()
            c_up(window, s).start()

    def forward_sides(window, s):
        y_up(window, s).wait_recv()
        f_low(window, s).start()
        y_down(window, s).wait_recv()
        f_high(window, s).start()

    def wait_rest(window, s):
        for b in range(boxes):
            s_copy(window, s, b).wait_recv()
        f_low(window, s).wait_recv()
        f_high(window, s).wait_recv()

        @pl.when(has_far)
        def _():
            for b in range(1, boxes - 1):
                x_copy(window, s, b).wait_recv()
            c_up(window, s).wait_recv()
            c_down(window, s).wait_recv()

    def wait_sends(window, s):
        for b in range(boxes):
            s_copy(window, s, b).wait_send()
        for copy in (y_up, y_down, f_low, f_high):
            copy(window, s).wait_send()

        @pl.when(has_far)
        def _():
            for b in range(boxes):
                x_copy(window, s, b).wait_send()
            c_up(window, s).wait_send()
            c_down(window, s).wait_send()

    @pl.when(jnp.logical_not(has_far))
    def _():
        for window in (*skel, *solved):
            def clear(i, carry, window=window):
                window[FAR * wide + i] = jnp.zeros(window.shape[1:], window.dtype)
                return carry

            lax.fori_loop(0, wide, clear, 0)

    lane = lax.broadcasted_iota(jnp.int32, (LANES, LANES), 1)

    def choose(b):
        blocks = []
        for ref, count in ((skel_idx, K), (red_idx, R)):
            names = ref[pl.ds(b, 1), :]
            for k in range(count // LANES):
                column = jnp.broadcast_to(names[:, k * LANES : (k + 1) * LANES], (LANES, LANES)).T
                pieces = [
                    jnp.where(column == lane + m * LANES, 1.0, 0.0).astype(jnp.bfloat16)
                    for m in range(M // LANES)
                ]
                blocks.append(jnp.concatenate(pieces, axis=1))
        return jnp.concatenate(blocks, axis=0)

    def gather(i, carry):
        b = lax.rem(3 * i, 4)
        load_fields(b).wait()
        taken = jnp.dot(choose(b), fields[b], preferred_element_type=jnp.float32).astype(jnp.bfloat16)
        for h in range(2):
            part = jnp.concatenate(
                [taken[:, h * half : (h + 1) * half], taken[:, (2 + h) * half : (3 + h) * half]], axis=1
            )
            skel[h][OWN * wide + 1 + b] = part[:K]
            redundant[h][b] = part[K:]
        return carry

    lax.fori_loop(0, boxes, gather, 0)

    pl.semaphore_wait(barrier, jnp.where(has_far, 4, 3))

    order = (0, 3, 2, 1)

    def send_x(window, s, which):
        @pl.when(has_far)
        def _():
            for b in which:
                x_copy(window, s, b).start()

    def send_skel(h, s):
        y_up(skel[h], s).start()
        y_down(skel[h], s).start()
        for b in range(boxes):
            s_copy(skel[h], s, b).start()

    def window_index(b, j):
        code = near[b, j]
        line = jnp.where(code >= 3, 1, 0) + jnp.where(code >= 6, 1, 0)
        place = jnp.where(line == 1, OWN, jnp.where(line == 2 * core, FAR, SIB))
        return place * wide + b + code - 3 * line

    def gathered(window, b):
        return jnp.concatenate([window[window_index(b, j)] for j in range(nearby)], axis=0)

    def solve(h, s):
        def body(i, carry):
            b = lax.rem(3 * i, 4)
            block = jnp.concatenate(
                [jnp.concatenate([coupling[b, part, j] for j in range(nearby)], axis=1) for part in range(2)], axis=0
            )
            product = jnp.dot(block, gathered(skel[h], b), preferred_element_type=jnp.float32)
            target = redundant[h][b].astype(jnp.float32) - to_complex(product, R, half)
            target_b = target.astype(jnp.bfloat16)
            full = jnp.dot(inverse[b].reshape(2 * R, R), target_b, preferred_element_type=jnp.float32)
            solved[h][OWN * wide + 1 + b] = to_complex(full, R, half).astype(jnp.bfloat16)

            @pl.when(has_far)
            def _():
                x_copy(solved[h], s, b).start()

            @pl.when(b == 0)
            def _():
                y_down(solved[h], s).start()

            @pl.when(b == boxes - 1)
            def _():
                y_up(solved[h], s).start()

            s_copy(solved[h], s, b).start()
            return carry

        lax.fori_loop(0, boxes, body, 0)

    def place(b):
        names = jnp.concatenate([skel_idx[pl.ds(b, 1), :], red_idx[pl.ds(b, 1), :]], axis=1)
        rows = lax.broadcasted_iota(jnp.int32, (M, M), 0)
        return jnp.where(rows == names, 1.0, 0.0).astype(jnp.bfloat16)

    def write(h, b, part):
        lanes = pl.ds((2 * part + h) * half, half)
        return pltpu.make_async_copy(result.at[b, :, lanes], out_hbm.at[b, :, lanes], out_sem.at[h, part, b])

    def renew(h, midway):
        def body(i, carry):
            b = lax.rem(3 * i, 4)
            block = jnp.concatenate(
                [jnp.concatenate([back[b, part, j] for j in range(nearby)], axis=1) for part in range(2)], axis=0
            )
            product = jnp.dot(block, gathered(solved[h], b), preferred_element_type=jnp.float32)
            kept = skel[h][OWN * wide + 1 + b].astype(jnp.float32) - to_complex(product, K, half)
            stacked = jnp.concatenate([kept.astype(jnp.bfloat16), solved[h][OWN * wide + 1 + b]], axis=0)
            placed = jnp.dot(place(b), stacked, preferred_element_type=jnp.float32).astype(jnp.bfloat16)
            for part in range(2):
                result[b, :, (2 * part + h) * half : (2 * part + h + 1) * half] = placed[
                    :, part * half : (part + 1) * half
                ]
                write(h, b, part).start()
            if midway is not None:
                @pl.when(i == 1)
                def _():
                    midway()
            return carry

        lax.fori_loop(0, boxes, body, 0)

    send_x(skel_0, 0, order)
    send_skel(0, 0)
    forward_corners(skel_0, 0)
    send_x(skel_1, 1, order)
    send_skel(1, 1)
    forward_sides(skel_0, 0)
    load_inverse.wait()
    load_coupling.wait()
    wait_rest(skel_0, 0)
    solve(0, 2)
    forward_corners(skel_1, 1)
    forward_sides(skel_1, 1)
    wait_rest(skel_1, 1)
    solve(1, 3)
    forward_corners(solved_0, 2)
    forward_sides(solved_0, 2)
    load_back.wait()
    wait_rest(solved_0, 2)

    def midway():
        forward_corners(solved_1, 3)
        forward_sides(solved_1, 3)

    renew(0, midway)
    wait_rest(solved_1, 3)
    renew(1, None)
    for s, window in enumerate((skel_0, skel_1, solved_0, solved_1)):
        wait_sends(window, s)
    for h in range(2):
        for b in range(boxes):
            for part in range(2):
                write(h, b, part).wait()


def on_device(
    rows_mesh, cols_mesh,
    fields, skeleton_index, redundant_index, neighbours, coupling, back_coupling, inverse,
):
    _, boxes, M, columns = fields.shape
    K, R, nearby = skeleton_index.shape[2], redundant_index.shape[2], neighbours.shape[2]
    bf16 = jnp.bfloat16
    wide = boxes + 2
    half = columns // 2
    anywhere = pl.BlockSpec(memory_space=pl.ANY)
    vmem = pl.BlockSpec(memory_space=pltpu.VMEM)
    dma = pltpu.SemaphoreType.DMA
    out = pl.pallas_call(
        functools.partial(kernel, (rows_mesh, cols_mesh, boxes, K, R, nearby)),
        out_shape=jax.ShapeDtypeStruct((boxes, M, columns), bf16),
        in_specs=[
            anywhere, vmem, vmem, pl.BlockSpec(memory_space=pltpu.SMEM), anywhere, anywhere, anywhere
        ],
        out_specs=anywhere,
        scratch_shapes=[
            pltpu.VMEM((boxes, M, columns), bf16),
            pltpu.VMEM((boxes, 2, nearby, R, K), bf16),
            pltpu.VMEM((boxes, 2, nearby, K, R), bf16),
            pltpu.VMEM((boxes, 2, R, R), bf16),
            pltpu.VMEM((boxes, R, half), bf16),
            pltpu.VMEM((boxes, R, half), bf16),
            pltpu.VMEM((3 * wide, K, half), bf16),
            pltpu.VMEM((3 * wide, K, half), bf16),
            pltpu.VMEM((3 * wide, R, half), bf16),
            pltpu.VMEM((3 * wide, R, half), bf16),
            pltpu.VMEM((boxes, M, columns), bf16),
            dma((3,)), dma((boxes,)), dma((2, 2, boxes)),
            dma((4, boxes)), dma((4, boxes)), dma((4, 2)), dma((4, 2)), dma((4, boxes)), dma((4, boxes)),
            dma((4, 2)), dma((4, 2)), dma((4, 2)), dma((4, 2)),
        ],
        compiler_params=pltpu.CompilerParams(
            collective_id=0, has_side_effects=True, vmem_limit_bytes=56 * 2**20
        ),
        cost_estimate=pl.CostEstimate(flops=14 * 10**9, bytes_accessed=25 * 10**6, transcendentals=0),
    )(
        fields.reshape(boxes, M, columns),
        skeleton_index.reshape(boxes, K),
        redundant_index.reshape(boxes, R),
        neighbours.reshape(boxes, nearby),
        coupling.reshape(boxes, 2, R, nearby, K).transpose(0, 1, 3, 2, 4),
        back_coupling.reshape(boxes, 2, K, nearby, R).transpose(0, 1, 3, 2, 4),
        inverse.reshape(boxes, 2, R, R),
    )
    return out.reshape(1, boxes, M, columns)


def solution(mesh):
    in_specs = (
        P("brow", "bcol", None, None),
        P("brow", "bcol", None),
        P("brow", "bcol", None),
        P("brow", "bcol", None),
        P("brow", "bcol", None, None, None, None),
        P("brow", "bcol", None, None, None, None),
        P("brow", "bcol", None, None, None),
    )
    out_specs = P("brow", "bcol", None, None)
    body = functools.partial(on_device, mesh.shape["brow"], mesh.shape["bcol"])
    return jax.shard_map(body, mesh=mesh, in_specs=in_specs, out_specs=out_specs, check_vma=False)
```

time: 452 us -> 69.1 us (0.15); the launches traced: 445 us -> 68.5 us
  local copies, waits for them, and re-layouts: 220 us -> 3.4 us
  loops' own time: 111 us -> 0 us
  Pallas kernels: 0 us -> 65 us
  matrix products: 33.1 us -> 0 us
  other arithmetic: 28.8 us -> 0 us
  waiting for transfers between devices: 28.8 us -> 0 us
  starting transfers between devices: 23.5 us -> 0 us
    while x44 -> x0, local copies, waits for them, and re-layouts: 120 us -> none
    another operation x2 -> x0, loops' own time: 111 us -> none  [the longest x1 55.4 us: on_device(): solved = lax.map(first, (box_ids, codes, c_flat, i_flat, red_flat))]
    pallas_call x0 -> x1, Pallas kernels: none -> 65 us  [on_device(): pl.pallas_call(functools.partial(kernel, (rows_mesh, cols_mesh, boxes, K,...]
    gather x7 -> x0, local copies, waits for them, and re-layouts: 63.3 us -> none  [the longest x2 29.9 us: on_device(): result = jnp.take_along_axis(stacked, inverse_order[..., None], axis=1)]
    dot_general x12 -> x0, matrix products: 33.1 us -> none  [the longest x4 15.2 us: first(): product = jnp.dot(block, window, preferred_element_type=jnp.float32)]
    ppermute x8 -> x0, waiting for transfers between devices: 28.8 us -> none  [the longest x4 27.1 us: padded_2(): lax.ppermute(lax.slice_in_dim(block, 0, width, axis=dim), axis, backward)]
    ppermute x8 -> x0, starting transfers between devices: 23.5 us -> none  [the longest x4 17.5 us: padded_2(): lax.ppermute(lax.slice_in_dim(block, 0, width, axis=dim), axis, backward)]
    concatenate x19 -> x0, other arithmetic: 12 us -> none  [the longest x2 9.21 us: padded_2(): block = jnp.concatenate([low, block, high], axis=dim)]
  transfers between devices with their start and end apart: 8 -> 0, of which waited for: 4 -> 0; matrix products, arithmetic and copies ran while one was open for 21% -> 0% of each run, Pallas kernels for 0% -> 0%
where the time goes in v1:
time: 69.1 us; the launch traced here: 68.5 us
  Pallas kernels  65 us (94%)
  local copies, waits for them, and re-layouts  3.4 us (5%)
    pallas_call x1, Pallas kernels, on_device(): pl.pallas_call(functools.partial(kernel, (rows_mesh, cols_mesh, boxes, K,...  65 us
    unnamed x1, local copies, waits for them, and re-layouts  3.4 us

profile of v1, /device:TPU:3, one launch (start us, length us, event | category | flops | bytes accessed | tf_op | source)
XLA Modules:
  0.0 68.5 jit_solution(2321354440779532901)
XLA Ops:
  0.0 65.0 %shard_map.73 = bf16[4,640,512]{2,1,0:T(8,128)(2,1)} custom-call(bf16[4,640,512]{2,1,0:T(8,128)(2,1)} %bitcast.15, s32[4,384]{1,0:T(4,128)} %bitcast.17, s32[4,256]{1,0:T(4,128)} %bitcast.18, s32[4,6]{1,0:T(4,128)} %bitcast.19, bf16[4,2,6,256,384]{4,3,2,1,0:T(8,128)(2,1)} %bitcast.13, bf16[4,2,6,384,256]{4,3,2,1,0:T(8,128)(2,1)} %bitcast.14, ...), custom_call_target="tpu_custom_call" | custom-call | flops 14000000000 | bytes 25000000 | tf_op jit(solution)/shard_map/pallas_call | solution.py:304
  65.0 3.4 %copy.9 = bf16[1,4,640,512]{3,2,1,0:T(8,128)(2,1)} copy(bf16[1,4,640,512]{3,2,1,0:T(8,128)(2,1)} %bitcast.12) | data formatting | bytes 5242880

commit v2 on v1

v2 whole, which is shorter than its diff:
```python
import functools

import jax
import jax.numpy as jnp
from jax import lax
from jax.experimental import pallas as pl
from jax.experimental.pallas import tpu as pltpu
from jax.sharding import PartitionSpec as P

MESH = pl.DeviceIdType.MESH
LANES = 128
OWN, SIB, FAR = 0, 1, 2


def to_complex(product, rows, half):
    real_part = product[:rows, :half] - product[rows:, half:]
    imag_part = product[:rows, half:] + product[rows:, :half]
    return jnp.concatenate([real_part, imag_part], axis=1)


def kernel(
    sizes,
    fields_hbm, skel_idx, red_idx, near, coupling_hbm, back_hbm, inverse_hbm,
    out_hbm,
    fields, coupling, back, inverse, skel, solved, placing, partial, slots,
    load_sem, field_sem, out_sem,
    x_send, x_recv, y_send, y_recv, s_send, s_recv, c_send, c_recv, f_send, f_recv,
):
    rows_mesh, cols_mesh, boxes, K, R, nearby = sizes
    M = K + R
    wide = boxes + 2
    window = 3 * wide
    last = boxes - 1
    half = LANES
    result = fields

    row, col = lax.axis_index("brow"), lax.axis_index("bcol")
    core = lax.rem(row, 2)
    sibling = row + 1 - 2 * core
    across = row - 1 + 2 * core
    has_far = jnp.logical_and(across >= 0, across < rows_mesh)
    up, down = lax.rem(col + 1, cols_mesh), lax.rem(col + cols_mesh - 1, cols_mesh)
    at_sibling, at_far, at_up, at_down = (sibling, col), (across, col), (row, up), (row, down)

    barrier = pltpu.get_barrier_semaphore()
    for device in (at_sibling, at_up, at_down):
        pl.semaphore_signal(barrier, inc=1, device_id=device, device_id_type=MESH)

    @pl.when(has_far)
    def _():
        pl.semaphore_signal(barrier, inc=1, device_id=at_far, device_id_type=MESH)

    def load_fields(b):
        return pltpu.make_async_copy(fields_hbm.at[b], fields.at[b], field_sem.at[b])

    for b in range(boxes):
        load_fields(b).start()
    named = pl.ds(0, nearby)
    load_inverse = pltpu.make_async_copy(inverse_hbm, inverse, load_sem.at[0])
    load_coupling = pltpu.make_async_copy(coupling_hbm, coupling.at[:, :, named], load_sem.at[1])
    load_back = pltpu.make_async_copy(back_hbm, back.at[:, :, named], load_sem.at[2])
    load_coupling.start()
    load_inverse.start()
    load_back.start()

    def remote(stage, source, target, device, send, recv):
        values, base = (skel, solved)[stage // 2], (stage % 2) * window
        return pltpu.make_async_remote_copy(
            src_ref=values.at[base + source], dst_ref=values.at[base + target], send_sem=send, recv_sem=recv,
            device_id=device, device_id_type=MESH,
        )

    def x_copy(s, b):
        return remote(s, OWN * wide + 1 + b, FAR * wide + 1 + b, at_far, x_send.at[s, b], x_recv.at[s, b])

    def y_up(s):
        return remote(s, OWN * wide + boxes, OWN * wide, at_up, y_send.at[s, 0], y_recv.at[s, 0])

    def y_down(s):
        return remote(s, OWN * wide + 1, OWN * wide + boxes + 1, at_down, y_send.at[s, 1], y_recv.at[s, 1])

    def s_copy(s, b):
        return remote(s, OWN * wide + 1 + b, SIB * wide + 1 + b, at_sibling, s_send.at[s, b], s_recv.at[s, b])

    def c_up(s):
        return remote(s, FAR * wide + boxes, FAR * wide, at_up, c_send.at[s, 0], c_recv.at[s, 0])

    def c_down(s):
        return remote(s, FAR * wide + 1, FAR * wide + boxes + 1, at_down, c_send.at[s, 1], c_recv.at[s, 1])

    def f_low(s):
        return remote(s, OWN * wide, SIB * wide, at_sibling, f_send.at[s, 0], f_recv.at[s, 0])

    def f_high(s):
        return remote(s, OWN * wide + last + 2, SIB * wide + last + 2, at_sibling, f_send.at[s, 1], f_recv.at[s, 1])

    def with_far(action):
        pl.when(has_far)(action)

    def send_x(s, which):
        @with_far
        def _():
            for b in which:
                x_copy(s, b).start()

    def arrive_x(s, which):
        @with_far
        def _():
            for b in which:
                x_copy(s, b).wait_recv()

    def corner_down(s):
        @with_far
        def _():
            x_copy(s, 0).wait_recv()
            c_down(s).start()

    def corner_up(s):
        @with_far
        def _():
            x_copy(s, last).wait_recv()
            c_up(s).start()

    def arrive_low_corner(s):
        with_far(lambda: c_up(s).wait_recv())

    def arrive_high_corner(s):
        with_far(lambda: c_down(s).wait_recv())

    def forward_sides(s):
        y_up(s).wait_recv()
        f_low(s).start()
        y_down(s).wait_recv()
        f_high(s).start()

    def arrive_sides(s):
        f_low(s).wait_recv()
        f_high(s).wait_recv()

    def send_y(s):
        y_up(s).start()
        y_down(s).start()

    def send_s(s):
        for b in range(boxes):
            s_copy(s, b).start()

    def arrive_s(s):
        for b in range(boxes):
            s_copy(s, b).wait_recv()

    def wait_sends(s):
        for b in range(boxes):
            s_copy(s, b).wait_send()
        for copy in (y_up, y_down, f_low, f_high):
            copy(s).wait_send()

        @with_far
        def _():
            for b in range(boxes):
                x_copy(s, b).wait_send()
            c_up(s).wait_send()
            c_down(s).wait_send()

    codes = (3, 2 * 3 * (1 - core), 2 * 3 * core)

    def find_slots(b, carry):
        for line in (OWN, SIB, FAR):
            for place in range(3):
                slot = nearby
                for j in range(nearby):
                    slot = jnp.where(near[b, j] == codes[line] + place, j, slot)
                slots[b, 3 * line + place] = slot
        for blocks in (coupling, back):
            for part in range(2):
                blocks[b, part, nearby] = jnp.zeros(blocks.shape[3:], blocks.dtype)
        return carry

    lax.fori_loop(0, boxes, find_slots, 0)

    @pl.when(jnp.logical_not(has_far))
    def _():
        def clear(i, carry):
            for h in range(2):
                for values in (skel, solved):
                    values[h * window + FAR * wide + i] = jnp.zeros(values.shape[1:], values.dtype)
            return carry

        lax.fori_loop(0, wide, clear, 0)

    lane = lax.broadcasted_iota(jnp.int32, (LANES, LANES), 1)

    def choose(b):
        blocks = []
        for ref, count in ((skel_idx, K), (red_idx, R)):
            names = ref[pl.ds(b, 1), :]
            for k in range(count // LANES):
                column = jnp.broadcast_to(names[:, k * LANES : (k + 1) * LANES], (LANES, LANES)).T
                pieces = [
                    jnp.where(column == lane + m * LANES, 1.0, 0.0).astype(jnp.bfloat16)
                    for m in range(M // LANES)
                ]
                blocks.append(jnp.concatenate(pieces, axis=1))
        return jnp.concatenate(blocks, axis=0)

    def gather(b, carry):
        load_fields(b).wait()
        taken = jnp.dot(choose(b), fields[b], preferred_element_type=jnp.float32)
        for h in range(2):
            part = jnp.concatenate(
                [taken[:, h * half : (h + 1) * half], taken[:, (2 + h) * half : (3 + h) * half]], axis=1
            )
            skel[h * window + OWN * wide + 1 + b] = part[:K].astype(jnp.bfloat16)
            partial[h * boxes + b, :R] = part[K:]
        return carry

    lax.fori_loop(0, boxes, gather, 0)

    def make_placing(b, carry):
        names = jnp.concatenate([skel_idx[pl.ds(b, 1), :], red_idx[pl.ds(b, 1), :]], axis=1)
        rows = lax.broadcasted_iota(jnp.int32, (M, M), 0)
        placing[b] = jnp.where(rows == names, 1.0, 0.0).astype(jnp.bfloat16)
        return carry

    def matrix(blocks, b, places):
        found = [slots[b, place] for place in places]
        return jnp.concatenate(
            [jnp.concatenate([blocks[b, part, slot] for slot in found], axis=1) for part in range(2)], axis=0
        )

    def line_values(values, h, line, b):
        three = values[pl.ds(h * window + line * wide + b, 3)]
        return three.reshape(3 * three.shape[1], three.shape[2])

    def near_part(blocks, values, h, b):
        own = h * window + OWN * wide + b
        vectors = jnp.concatenate([values[own], values[own + 2], line_values(values, h, SIB, b)], axis=0)
        places = (3 * OWN, 3 * OWN + 2, 3 * SIB, 3 * SIB + 1, 3 * SIB + 2)
        product = jnp.dot(matrix(blocks, b, places), vectors, preferred_element_type=jnp.float32)
        return to_complex(product, product.shape[0] // 2, half)

    def far_part(blocks, values, h, b):
        places = (3 * FAR, 3 * FAR + 1, 3 * FAR + 2)
        product = jnp.dot(
            matrix(blocks, b, places), line_values(values, h, FAR, b), preferred_element_type=jnp.float32
        )
        return to_complex(product, product.shape[0] // 2, half)

    def solve_near(h, b):
        partial[h * boxes + b, :R] -= near_part(coupling, skel, h, b)

    def solve_far(h, b):
        target = partial[h * boxes + b, :R] - far_part(coupling, skel, h, b)
        full = jnp.dot(
            inverse[b].reshape(2 * R, R), target.astype(jnp.bfloat16), preferred_element_type=jnp.float32
        )
        solved[h * window + OWN * wide + 1 + b] = to_complex(full, R, half).astype(jnp.bfloat16)

    def renew_near(h, b):
        kept = skel[h * window + OWN * wide + 1 + b].astype(jnp.float32)
        partial[h * boxes + b] = kept - near_part(back, solved, h, b)

    def write(h, b, part):
        lanes = pl.ds((2 * part + h) * half, half)
        return pltpu.make_async_copy(result.at[b, :, lanes], out_hbm.at[b, :, lanes], out_sem.at[h, part, b])

    def renew_far(h, b):
        renewed = partial[h * boxes + b] - far_part(back, solved, h, b)
        stacked = jnp.concatenate(
            [renewed.astype(jnp.bfloat16), solved[h * window + OWN * wide + 1 + b]], axis=0
        )
        placed = jnp.dot(placing[b], stacked, preferred_element_type=jnp.float32).astype(jnp.bfloat16)
        for part in range(2):
            result[b, :, (2 * part + h) * half : (2 * part + h + 1) * half] = placed[
                :, part * half : (part + 1) * half
            ]
            write(h, b, part).start()

    def inner(work, h):
        def body(i, carry):
            work(h, 1 + i)
            return carry

        lax.fori_loop(0, 2, body, 0)

    def outer(work, h):
        def body(i, carry):
            work(h, last * i)
            return carry

        lax.fori_loop(0, 2, body, 0)

    def in_order(work, h, order, before):
        def body(i, carry):
            b = sum(jnp.where(i == k, order[k], 0) for k in range(1, boxes)) + jnp.where(i == 0, order[0], 0)
            for k, action in before.items():
                pl.when(i == k)(action)
            work(h, b)
            return carry

        lax.fori_loop(0, boxes, body, 0)

    pl.semaphore_wait(barrier, jnp.where(has_far, 4, 3))

    send_x(0, (0, last, 1, 2))
    send_y(0)
    send_s(0)
    send_s(1)
    lax.fori_loop(0, boxes, make_placing, 0)
    load_coupling.wait()
    arrive_s(0)
    inner(solve_near, 0)
    corner_down(0)
    arrive_s(1)
    inner(solve_near, 1)
    corner_up(0)
    send_x(1, (0, last))
    forward_sides(0)
    send_y(1)
    arrive_sides(0)
    outer(solve_near, 0)
    arrive_x(0, (1, 2))
    send_x(1, (1, 2))
    load_inverse.wait()

    def before_first():
        arrive_low_corner(0)

    def before_last():
        corner_down(1)
        arrive_high_corner(0)

    in_order(solve_far, 0, (1, 2, 0, last), {2: before_first, 3: before_last})
    send_s(2)
    corner_up(1)
    send_x(2, (0, last, 1, 2))
    send_y(2)
    forward_sides(1)
    load_back.wait()
    arrive_s(2)
    inner(renew_near, 0)
    arrive_sides(1)
    outer(solve_near, 1)
    arrive_x(1, (1, 2))

    def before_low():
        arrive_low_corner(1)

    def after_low():
        send_x(3, (0,))
        y_down(3).start()
        corner_down(2)

    def before_high():
        arrive_high_corner(1)

    in_order(solve_far, 1, (1, 0, 2, last), {1: before_low, 2: after_low, 3: before_high})
    send_x(3, (last, 1, 2))
    y_up(3).start()
    send_s(3)
    corner_up(2)
    forward_sides(2)
    arrive_s(3)
    inner(renew_near, 1)
    arrive_sides(2)
    outer(renew_near, 0)
    corner_down(3)
    arrive_x(2, (1, 2))

    def before_rims():
        corner_up(3)
        arrive_low_corner(2)
        arrive_high_corner(2)

    in_order(renew_far, 0, (1, 2, 0, last), {2: before_rims})
    forward_sides(3)
    arrive_x(3, (1, 2))
    inner(renew_far, 1)
    arrive_sides(3)
    outer(renew_near, 1)
    arrive_low_corner(3)
    arrive_high_corner(3)
    outer(renew_far, 1)
    for s in range(4):
        wait_sends(s)
    for h in range(2):
        for b in range(boxes):
            for part in range(2):
                write(h, b, part).wait()


def on_device(
    rows_mesh, cols_mesh,
    fields, skeleton_index, redundant_index, neighbours, coupling, back_coupling, inverse,
):
    _, boxes, M, columns = fields.shape
    K, R, nearby = skeleton_index.shape[2], redundant_index.shape[2], neighbours.shape[2]
    bf16 = jnp.bfloat16
    wide = boxes + 2
    half = columns // 2
    anywhere = pl.BlockSpec(memory_space=pl.ANY)
    vmem = pl.BlockSpec(memory_space=pltpu.VMEM)
    dma = pltpu.SemaphoreType.DMA
    out = pl.pallas_call(
        functools.partial(kernel, (rows_mesh, cols_mesh, boxes, K, R, nearby)),
        out_shape=jax.ShapeDtypeStruct((boxes, M, columns), bf16),
        in_specs=[
            anywhere, vmem, vmem, pl.BlockSpec(memory_space=pltpu.SMEM), anywhere, anywhere, anywhere
        ],
        out_specs=anywhere,
        scratch_shapes=[
            pltpu.VMEM((boxes, M, columns), bf16),
            pltpu.VMEM((boxes, 2, nearby + 1, R, K), bf16),
            pltpu.VMEM((boxes, 2, nearby + 1, K, R), bf16),
            pltpu.VMEM((boxes, 2, R, R), bf16),
            pltpu.VMEM((2 * 3 * wide, K, half), bf16),
            pltpu.VMEM((2 * 3 * wide, R, half), bf16),
            pltpu.VMEM((boxes, M, M), bf16),
            pltpu.VMEM((2 * boxes, K, half), jnp.float32),
            pltpu.SMEM((boxes, 9), jnp.int32),
            dma((3,)), dma((boxes,)), dma((2, 2, boxes)),
            dma((4, boxes)), dma((4, boxes)), dma((4, 2)), dma((4, 2)), dma((4, boxes)), dma((4, boxes)),
            dma((4, 2)), dma((4, 2)), dma((4, 2)), dma((4, 2)),
        ],
        compiler_params=pltpu.CompilerParams(
            collective_id=0, has_side_effects=True, vmem_limit_bytes=48 * 2**20
        ),
        cost_estimate=pl.CostEstimate(flops=14 * 10**9, bytes_accessed=25 * 10**6, transcendentals=0),
    )(
        fields.reshape(boxes, M, columns),
        skeleton_index.reshape(boxes, K),
        redundant_index.reshape(boxes, R),
        neighbours.reshape(boxes, nearby),
        coupling.reshape(boxes, 2, R, nearby, K).transpose(0, 1, 3, 2, 4),
        back_coupling.reshape(boxes, 2, K, nearby, R).transpose(0, 1, 3, 2, 4),
        inverse.reshape(boxes, 2, R, R),
    )
    return out.reshape(1, boxes, M, columns)


def solution(mesh):
    in_specs = (
        P("brow", "bcol", None, None),
        P("brow", "bcol", None),
        P("brow", "bcol", None),
        P("brow", "bcol", None),
        P("brow", "bcol", None, None, None, None),
        P("brow", "bcol", None, None, None, None),
        P("brow", "bcol", None, None, None),
    )
    out_specs = P("brow", "bcol", None, None)
    body = functools.partial(on_device, mesh.shape["brow"], mesh.shape["bcol"])
    return jax.shard_map(body, mesh=mesh, in_specs=in_specs, out_specs=out_specs, check_vma=False)
```

time: 69.1 us -> 58.1 us (0.84)
  Pallas kernels: 65 us -> 52.2 us
  local copies, waits for them, and re-layouts: 3.4 us -> 4.78 us
    pallas_call x1, Pallas kernels: 65 us -> 52.2 us  [on_device(): pl.pallas_call(functools.partial(kernel, (rows_mesh, cols_mesh, boxes, K,...]
    unnamed x1 -> x9, local copies, waits for them, and re-layouts: 3.4 us -> 4.78 us
where the time goes in v2:
time: 58.1 us; the launch traced here: 57 us
  Pallas kernels  52.2 us (90%)
  local copies, waits for them, and re-layouts  4.78 us (8%)
    pallas_call x1, Pallas kernels, on_device(): pl.pallas_call(functools.partial(kernel, (rows_mesh, cols_mesh, boxes, K,...  52.2 us
    unnamed x9, local copies, waits for them, and re-layouts  4.78 us

profile of v2, /device:TPU:3, one launch (start us, length us, event | category | flops | bytes accessed | tf_op | source)
XLA Modules:
  0.0 57.0 jit_solution(1018056722985056104)
XLA Ops:
  0.0 0.0 copy-start
  0.0 1.2 %copy-done = bf16[1,4,2,256,256]{4,3,2,1,0:T(8,128)(2,1)S(1)} copy-done((bf16[1,4,2,256,256]{4,3,2,1,0:T(8,128)(2,1)S(1)}, bf16[1,4,2,256,256]{4,3,2,1,0:T(8,128)(2,1)}, u32[]{:S(2)}) %copy-start) | copy-done | bytes 1048600
  1.2 0.0 copy-start.1
  1.2 0.7 %copy-done.1 = s32[1,4,384]{2,1,0:T(4,128)S(1)} copy-done((s32[1,4,384]{2,1,0:T(4,128)S(1)}, s32[1,4,384]{2,1,0:T(4,128)}, u32[]{:S(2)}) %copy-start.1) | copy-done | bytes 6168
  1.9 0.0 copy-start.2
  1.9 0.7 %copy-done.2 = s32[1,4,256]{2,1,0:T(4,128)S(1)} copy-done((s32[1,4,256]{2,1,0:T(4,128)S(1)}, s32[1,4,256]{2,1,0:T(4,128)}, u32[]{:S(2)}) %copy-start.2) | copy-done | bytes 4120
  2.6 0.0 copy-start.3
  2.6 0.7 %copy-done.3 = s32[1,4,6]{2,1,0:T(4,128)S(1)} copy-done((s32[1,4,6]{2,1,0:T(4,128)S(1)}, s32[1,4,6]{2,1,0:T(4,128)}, u32[]{:S(2)}) %copy-start.3) | copy-done | bytes 120
  3.3 52.2 %shard_map.73 = bf16[4,640,512]{2,1,0:T(8,128)(2,1)S(1)} custom-call(bf16[4,640,512]{2,1,0:T(8,128)(2,1)} %bitcast.19, s32[4,384]{1,0:T(4,128)S(1)} %bitcast.14, s32[4,256]{1,0:T(4,128)S(1)} %bitcast.15, s32[4,6]{1,0:T(4,128)S(1)} %bitcast.16, bf16[4,2,6,256,384]{4,3,2,1,0:T(8,128)(2,1)} %bitcast.17, bf16[4,2,6,384,256]{4,3,2,1,0:T(8,128)(2,1)} %bitcast.18, ...), custom_call_target="tpu_custom_call" | custom-call | flops 14000000000 | bytes 25000000 | tf_op jit(solution)/shard_map/pallas_call | solution.py:404
  55.5 1.5 %copy.9 = bf16[1,4,640,512]{3,2,1,0:T(8,128)(2,1)} copy(bf16[1,4,640,512]{3,2,1,0:T(8,128)(2,1)S(1)} %bitcast.12) | data formatting | bytes 5242880
Async XLA Ops:
  0.0 1.2 %copy-start = (bf16[1,4,2,256,256]{4,3,2,1,0:T(8,128)(2,1)S(1)}, bf16[1,4,2,256,256]{4,3,2,1,0:T(8,128)(2,1)}, u32[]{:S(2)}) copy-start(bf16[1,4,2,256,256]{4,3,2,1,0:T(8,128)(2,1)} %param.13) | copy-start | bytes 3145732
  1.2 0.7 %copy-start.1 = (s32[1,4,384]{2,1,0:T(4,128)S(1)}, s32[1,4,384]{2,1,0:T(4,128)}, u32[]{:S(2)}) copy-start(s32[1,4,384]{2,1,0:T(4,128)} %param.8) | copy-start | bytes 18436
  1.9 0.7 %copy-start.2 = (s32[1,4,256]{2,1,0:T(4,128)S(1)}, s32[1,4,256]{2,1,0:T(4,128)}, u32[]{:S(2)}) copy-start(s32[1,4,256]{2,1,0:T(4,128)} %param.9) | copy-start | bytes 12292
  2.6 0.7 %copy-start.3 = (s32[1,4,6]{2,1,0:T(4,128)S(1)}, s32[1,4,6]{2,1,0:T(4,128)}, u32[]{:S(2)}) copy-start(s32[1,4,6]{2,1,0:T(4,128)} %param.10) | copy-start | bytes 292

commit v3 on v2

--- a/solution.py
+++ b/solution.py
@@ -20,10 +20,10 @@
 
 def kernel(
     sizes,
-    fields_hbm, skel_idx, red_idx, near, coupling_hbm, back_hbm, inverse_hbm,
-    out_hbm,
-    fields, coupling, back, inverse, skel, solved, placing, partial, slots,
-    load_sem, field_sem, out_sem,
+    fields_hbm, skel_hbm, red_hbm, near_hbm, coupling_hbm, back_hbm, inverse_hbm,
+    result,
+    fields, skel_idx, red_idx, near, coupling, back, inverse, skel, solved, placing, partial, slots,
+    load_sem, field_sem,
     x_send, x_recv, y_send, y_recv, s_send, s_recv, c_send, c_recv, f_send, f_recv,
 ):
     rows_mesh, cols_mesh, boxes, K, R, nearby = sizes
@@ -32,7 +32,6 @@
     window = 3 * wide
     last = boxes - 1
     half = LANES
-    result = fields
 
     row, col = lax.axis_index("brow"), lax.axis_index("bcol")
     core = lax.rem(row, 2)
@@ -53,6 +52,12 @@
     def load_fields(b):
         return pltpu.make_async_copy(fields_hbm.at[b], fields.at[b], field_sem.at[b])
 
+    loads = [
+        pltpu.make_async_copy(source, target, load_sem.at[3 + k])
+        for k, (source, target) in enumerate(((skel_hbm, skel_idx), (red_hbm, red_idx), (near_hbm, near)))
+    ]
+    for load in loads:
+        load.start()
     for b in range(boxes):
         load_fields(b).start()
     named = pl.ds(0, nearby)
@@ -176,6 +181,8 @@
                 blocks[b, part, nearby] = jnp.zeros(blocks.shape[3:], blocks.dtype)
         return carry
 
+    for load in loads:
+        load.wait()
     lax.fori_loop(0, boxes, find_slots, 0)
 
     @pl.when(jnp.logical_not(has_far))
@@ -246,59 +253,36 @@
         )
         return to_complex(product, product.shape[0] // 2, half)
 
-    def solve_near(h, b):
-        partial[h * boxes + b, :R] -= near_part(coupling, skel, h, b)
-
-    def solve_far(h, b):
-        target = partial[h * boxes + b, :R] - far_part(coupling, skel, h, b)
-        full = jnp.dot(
-            inverse[b].reshape(2 * R, R), target.astype(jnp.bfloat16), preferred_element_type=jnp.float32
-        )
-        solved[h * window + OWN * wide + 1 + b] = to_complex(full, R, half).astype(jnp.bfloat16)
-
-    def renew_near(h, b):
-        kept = skel[h * window + OWN * wide + 1 + b].astype(jnp.float32)
-        partial[h * boxes + b] = kept - near_part(back, solved, h, b)
-
-    def write(h, b, part):
-        lanes = pl.ds((2 * part + h) * half, half)
-        return pltpu.make_async_copy(result.at[b, :, lanes], out_hbm.at[b, :, lanes], out_sem.at[h, part, b])
-
-    def renew_far(h, b):
-        renewed = partial[h * boxes + b] - far_part(back, solved, h, b)
-        stacked = jnp.concatenate(
-            [renewed.astype(jnp.bfloat16), solved[h * window + OWN * wide + 1 + b]], axis=0
-        )
-        placed = jnp.dot(placing[b], stacked, preferred_element_type=jnp.float32).astype(jnp.bfloat16)
-        for part in range(2):
-            result[b, :, (2 * part + h) * half : (2 * part + h + 1) * half] = placed[
-                :, part * half : (part + 1) * half
-            ]
-            write(h, b, part).start()
-
-    def inner(work, h):
-        def body(i, carry):
-            work(h, 1 + i)
-            return carry
-
-        lax.fori_loop(0, 2, body, 0)
-
-    def outer(work, h):
-        def body(i, carry):
-            work(h, last * i)
-            return carry
-
-        lax.fori_loop(0, 2, body, 0)
-
-    def in_order(work, h, order, before):
-        def body(i, carry):
-            b = sum(jnp.where(i == k, order[k], 0) for k in range(1, boxes)) + jnp.where(i == 0, order[0], 0)
-            for k, action in before.items():
-                pl.when(i == k)(action)
-            work(h, b)
-            return carry
-
-        lax.fori_loop(0, boxes, body, 0)
+    def solve_near(h, bs):
+        for b in bs:
+            partial[h * boxes + b, :R] -= near_part(coupling, skel, h, b)
+
+    def solve_far(h, bs):
+        targets = [
+            (partial[h * boxes + b, :R] - far_part(coupling, skel, h, b)).astype(jnp.bfloat16) for b in bs
+        ]
+        for b, target in zip(bs, targets):
+            full = jnp.dot(inverse[b].reshape(2 * R, R), target, preferred_element_type=jnp.float32)
+            solved[h * window + OWN * wide + 1 + b] = to_complex(full, R, half).astype(jnp.bfloat16)
+
+    def renew_near(h, bs):
+        for b in bs:
+            kept = skel[h * window + OWN * wide + 1 + b].astype(jnp.float32)
+            partial[h * boxes + b] = kept - near_part(back, solved, h, b)
+
+    def renew_far(h, bs):
+        renewed = [
+            (partial[h * boxes + b] - far_part(back, solved, h, b)).astype(jnp.bfloat16) for b in bs
+        ]
+        for b, kept in zip(bs, renewed):
+            stacked = jnp.concatenate([kept, solved[h * window + OWN * wide + 1 + b]], axis=0)
+            placed = jnp.dot(placing[b], stacked, preferred_element_type=jnp.float32).astype(jnp.bfloat16)
+            for part in range(2):
+                result[b, :, (2 * part + h) * half : (2 * part + h + 1) * half] = placed[
+                    :, part * half : (part + 1) * half
+                ]
+
+    inner, outer = (1, 2), (0, last)
 
     pl.semaphore_wait(barrier, jnp.where(has_far, 4, 3))
 
@@ -309,28 +293,24 @@
     lax.fori_loop(0, boxes, make_placing, 0)
     load_coupling.wait()
     arrive_s(0)
-    inner(solve_near, 0)
+    solve_near(0, inner)
     corner_down(0)
     arrive_s(1)
-    inner(solve_near, 1)
+    solve_near(1, inner)
     corner_up(0)
-    send_x(1, (0, last))
+    send_x(1, outer)
     forward_sides(0)
     send_y(1)
     arrive_sides(0)
-    outer(solve_near, 0)
-    arrive_x(0, (1, 2))
-    send_x(1, (1, 2))
+    solve_near(0, outer)
+    arrive_x(0, inner)
+    send_x(1, inner)
     load_inverse.wait()
-
-    def before_first():
-        arrive_low_corner(0)
-
-    def before_last():
-        corner_down(1)
-        arrive_high_corner(0)
-
-    in_order(solve_far, 0, (1, 2, 0, last), {2: before_first, 3: before_last})
+    solve_far(0, inner)
+    corner_down(1)
+    arrive_low_corner(0)
+    arrive_high_corner(0)
+    solve_far(0, outer)
     send_s(2)
     corner_up(1)
     send_x(2, (0, last, 1, 2))
@@ -338,55 +318,42 @@
     forward_sides(1)
     load_back.wait()
     arrive_s(2)
-    inner(renew_near, 0)
+    renew_near(0, inner)
     arrive_sides(1)
-    outer(solve_near, 1)
-    arrive_x(1, (1, 2))
-
-    def before_low():
-        arrive_low_corner(1)
-
-    def after_low():
-        send_x(3, (0,))
-        y_down(3).start()
-        corner_down(2)
-
-    def before_high():
-        arrive_high_corner(1)
-
-    in_order(solve_far, 1, (1, 0, 2, last), {1: before_low, 2: after_low, 3: before_high})
-    send_x(3, (last, 1, 2))
-    y_up(3).start()
+    solve_near(1, outer)
+    arrive_x(1, inner)
+    solve_far(1, inner)
+    send_x(3, (1,))
+    corner_down(2)
+    arrive_low_corner(1)
+    arrive_high_corner(1)
+    solve_far(1, outer)
+    send_x(3, (0, last, 2))
     send_s(3)
     corner_up(2)
+    send_y(3)
     forward_sides(2)
     arrive_s(3)
-    inner(renew_near, 1)
+    renew_near(1, inner)
     arrive_sides(2)
-    outer(renew_near, 0)
+    renew_near(0, outer)
     corner_down(3)
-    arrive_x(2, (1, 2))
-
-    def before_rims():
-        corner_up(3)
-        arrive_low_corner(2)
-        arrive_high_corner(2)
-
-    in_order(renew_far, 0, (1, 2, 0, last), {2: before_rims})
+    arrive_x(2, inner)
+    renew_far(0, inner)
+    corner_up(3)
+    arrive_low_corner(2)
+    arrive_high_corner(2)
+    renew_far(0, outer)
     forward_sides(3)
-    arrive_x(3, (1, 2))
-    inner(renew_far, 1)
+    arrive_x(3, inner)
+    renew_far(1, inner)
     arrive_sides(3)
-    outer(renew_near, 1)
+    renew_near(1, outer)
     arrive_low_corner(3)
     arrive_high_corner(3)
-    outer(renew_far, 1)
+    renew_far(1, outer)
     for s in range(4):
         wait_sends(s)
-    for h in range(2):
-        for b in range(boxes):
-            for part in range(2):
-                write(h, b, part).wait()
 
 
 def on_device(
@@ -398,18 +365,18 @@
     bf16 = jnp.bfloat16
     wide = boxes + 2
     half = columns // 2
-    anywhere = pl.BlockSpec(memory_space=pl.ANY)
-    vmem = pl.BlockSpec(memory_space=pltpu.VMEM)
+    far_memory = pl.BlockSpec(memory_space=pltpu.HBM)
     dma = pltpu.SemaphoreType.DMA
     out = pl.pallas_call(
         functools.partial(kernel, (rows_mesh, cols_mesh, boxes, K, R, nearby)),
-        out_shape=jax.ShapeDtypeStruct((boxes, M, columns), bf16),
-        in_specs=[
-            anywhere, vmem, vmem, pl.BlockSpec(memory_space=pltpu.SMEM), anywhere, anywhere, anywhere
-        ],
-        out_specs=anywhere,
+        out_shape=pltpu.VMEM((boxes, M, columns), bf16),
+        in_specs=[far_memory] * 7,
+        out_specs=pl.BlockSpec(memory_space=pltpu.VMEM),
         scratch_shapes=[
             pltpu.VMEM((boxes, M, columns), bf16),
+            pltpu.VMEM((boxes, K), jnp.int32),
+            pltpu.VMEM((boxes, R), jnp.int32),
+            pltpu.SMEM((boxes, nearby), jnp.int32),
             pltpu.VMEM((boxes, 2, nearby + 1, R, K), bf16),
             pltpu.VMEM((boxes, 2, nearby + 1, K, R), bf16),
             pltpu.VMEM((boxes, 2, R, R), bf16),
@@ -418,12 +385,12 @@
             pltpu.VMEM((boxes, M, M), bf16),
             pltpu.VMEM((2 * boxes, K, half), jnp.float32),
             pltpu.SMEM((boxes, 9), jnp.int32),
-            dma((3,)), dma((boxes,)), dma((2, 2, boxes)),
+            dma((6,)), dma((boxes,)),
             dma((4, boxes)), dma((4, boxes)), dma((4, 2)), dma((4, 2)), dma((4, boxes)), dma((4, boxes)),
             dma((4, 2)), dma((4, 2)), dma((4, 2)), dma((4, 2)),
         ],
         compiler_params=pltpu.CompilerParams(
-            collective_id=0, has_side_effects=True, vmem_limit_bytes=48 * 2**20
+            collective_id=0, has_side_effects=True, vmem_limit_bytes=56 * 2**20
         ),
         cost_estimate=pl.CostEstimate(flops=14 * 10**9, bytes_accessed=25 * 10**6, transcendentals=0),
     )(

time: 58.1 us -> 48.9 us (0.84); the launches traced: 57 us -> 48.6 us
  Pallas kernels: 52.2 us -> 47.1 us
  local copies, waits for them, and re-layouts: 4.78 us -> 1.49 us
    pallas_call x1, Pallas kernels: 52.2 us -> 47.1 us  [on_device(): pl.pallas_call(functools.partial(kernel, (rows_mesh, cols_mesh, boxes, K,...]
    unnamed x9 -> x1, local copies, waits for them, and re-layouts: 4.78 us -> 1.49 us
where the time goes in v3:
time: 48.9 us; the launch traced here: 48.6 us
  Pallas kernels  47.1 us (96%)
  local copies, waits for them, and re-layouts  1.49 us (3%)
    pallas_call x1, Pallas kernels, on_device(): pl.pallas_call(functools.partial(kernel, (rows_mesh, cols_mesh, boxes, K,...  47.1 us
    unnamed x1, local copies, waits for them, and re-layouts  1.49 us

profile of v3, /device:TPU:3, one launch (start us, length us, event | category | flops | bytes accessed | tf_op | source)
XLA Modules:
  0.0 48.6 jit_solution(9782226509106245251)
XLA Ops:
  0.0 47.1 %shard_map.73 = bf16[4,640,512]{2,1,0:T(8,128)(2,1)S(1)} custom-call(bf16[4,640,512]{2,1,0:T(8,128)(2,1)} %bitcast.15, s32[4,384]{1,0:T(4,128)} %bitcast.17, s32[4,256]{1,0:T(4,128)} %bitcast.18, s32[4,6]{1,0:T(4,128)} %bitcast.19, bf16[4,2,6,256,384]{4,3,2,1,0:T(8,128)(2,1)} %bitcast.13, bf16[4,2,6,384,256]{4,3,2,1,0:T(8,128)(2,1)} %bitcast.14, ...), custom_call_target="tpu_custom_call" | custom-call | flops 14000000000 | bytes 25000000 | tf_op jit(solution)/shard_map/pallas_call | solution.py:370
  47.1 1.5 %copy.9 = bf16[1,4,640,512]{3,2,1,0:T(8,128)(2,1)} copy(bf16[1,4,640,512]{3,2,1,0:T(8,128)(2,1)S(1)} %bitcast.12) | data formatting | bytes 5242880

commit v4 on v3

--- a/solution.py
+++ b/solution.py
@@ -58,7 +58,8 @@
     ]
     for load in loads:
         load.start()
-    for b in range(boxes):
+    inner, outer = (1, 2), (0, last)
+    for b in (*outer, *inner):
         load_fields(b).start()
     named = pl.ds(0, nearby)
     load_inverse = pltpu.make_async_copy(inverse_hbm, inverse, load_sem.at[0])
@@ -146,8 +147,8 @@
         y_up(s).start()
         y_down(s).start()
 
-    def send_s(s):
-        for b in range(boxes):
+    def send_s(s, which):
+        for b in which:
             s_copy(s, b).start()
 
     def arrive_s(s):
@@ -181,12 +182,8 @@
                 blocks[b, part, nearby] = jnp.zeros(blocks.shape[3:], blocks.dtype)
         return carry
 
-    for load in loads:
-        load.wait()
-    lax.fori_loop(0, boxes, find_slots, 0)
-
-    @pl.when(jnp.logical_not(has_far))
-    def _():
+
+    def clear_far():
         def clear(i, carry):
             for h in range(2):
                 for values in (skel, solved):
@@ -197,31 +194,52 @@
 
     lane = lax.broadcasted_iota(jnp.int32, (LANES, LANES), 1)
 
-    def choose(b):
+    def choose(ref, count, b):
         blocks = []
-        for ref, count in ((skel_idx, K), (red_idx, R)):
-            names = ref[pl.ds(b, 1), :]
-            for k in range(count // LANES):
-                column = jnp.broadcast_to(names[:, k * LANES : (k + 1) * LANES], (LANES, LANES)).T
-                pieces = [
-                    jnp.where(column == lane + m * LANES, 1.0, 0.0).astype(jnp.bfloat16)
-                    for m in range(M // LANES)
-                ]
-                blocks.append(jnp.concatenate(pieces, axis=1))
+        names = ref[pl.ds(b, 1), :]
+        for k in range(count // LANES):
+            column = jnp.broadcast_to(names[:, k * LANES : (k + 1) * LANES], (LANES, LANES)).T
+            pieces = [
+                jnp.where(column == lane + m * LANES, 1.0, 0.0).astype(jnp.bfloat16) for m in range(M // LANES)
+            ]
+            blocks.append(jnp.concatenate(pieces, axis=1))
         return jnp.concatenate(blocks, axis=0)
 
-    def gather(b, carry):
-        load_fields(b).wait()
-        taken = jnp.dot(choose(b), fields[b], preferred_element_type=jnp.float32)
+    def halves(taken):
         for h in range(2):
-            part = jnp.concatenate(
+            yield h, jnp.concatenate(
                 [taken[:, h * half : (h + 1) * half], taken[:, (2 + h) * half : (3 + h) * half]], axis=1
             )
-            skel[h * window + OWN * wide + 1 + b] = part[:K].astype(jnp.bfloat16)
-            partial[h * boxes + b, :R] = part[K:]
+
+    def gather_skeleton(b):
+        chosen = choose(skel_idx, K, b)
+        load_fields(b).wait()
+        taken = jnp.dot(chosen, fields[b], preferred_element_type=jnp.float32)
+        for h, part in halves(taken):
+            skel[h * window + OWN * wide + 1 + b] = part.astype(jnp.bfloat16)
+
+    def gather_outer(i, carry):
+        b = last * i
+        gather_skeleton(b)
+
+        @pl.when(i == 0)
+        def _():
+            pl.semaphore_wait(barrier, jnp.where(has_far, 4, 3))
+            y_down(0).start()
+
+        with_far(lambda: x_copy(0, b).start())
+        pl.when(i == 1)(lambda: y_up(0).start())
         return carry
 
-    lax.fori_loop(0, boxes, gather, 0)
+    def gather_inner(i, carry):
+        gather_skeleton(1 + i)
+        return carry
+
+    def gather_redundant(b, carry):
+        taken = jnp.dot(choose(red_idx, R, b), fields[b], preferred_element_type=jnp.float32)
+        for h, part in halves(taken):
+            partial[h * boxes + b, :R] = part
+        return carry
 
     def make_placing(b, carry):
         names = jnp.concatenate([skel_idx[pl.ds(b, 1), :], red_idx[pl.ds(b, 1), :]], axis=1)
@@ -235,22 +253,21 @@
             [jnp.concatenate([blocks[b, part, slot] for slot in found], axis=1) for part in range(2)], axis=0
         )
 
-    def line_values(values, h, line, b):
-        three = values[pl.ds(h * window + line * wide + b, 3)]
-        return three.reshape(3 * three.shape[1], three.shape[2])
+    def line_values(values, h, line, place, count):
+        found = values[pl.ds(h * window + line * wide + place, count)]
+        return found.reshape(count * found.shape[1], found.shape[2])
 
     def near_part(blocks, values, h, b):
         own = h * window + OWN * wide + b
-        vectors = jnp.concatenate([values[own], values[own + 2], line_values(values, h, SIB, b)], axis=0)
+        vectors = jnp.concatenate([values[own], values[own + 2], line_values(values, h, SIB, b, 3)], axis=0)
         places = (3 * OWN, 3 * OWN + 2, 3 * SIB, 3 * SIB + 1, 3 * SIB + 2)
         product = jnp.dot(matrix(blocks, b, places), vectors, preferred_element_type=jnp.float32)
         return to_complex(product, product.shape[0] // 2, half)
 
-    def far_part(blocks, values, h, b):
-        places = (3 * FAR, 3 * FAR + 1, 3 * FAR + 2)
-        product = jnp.dot(
-            matrix(blocks, b, places), line_values(values, h, FAR, b), preferred_element_type=jnp.float32
-        )
+    def far_part(blocks, values, h, b, first=0, count=3):
+        places = [3 * FAR + first + k for k in range(count)]
+        vectors = line_values(values, h, FAR, b + first, count)
+        product = jnp.dot(matrix(blocks, b, places), vectors, preferred_element_type=jnp.float32)
         return to_complex(product, product.shape[0] // 2, half)
 
     def solve_near(h, bs):
@@ -270,10 +287,18 @@
             kept = skel[h * window + OWN * wide + 1 + b].astype(jnp.float32)
             partial[h * boxes + b] = kept - near_part(back, solved, h, b)
 
+    def renew_sides(h):
+        for b in outer:
+            partial[h * boxes + b] -= far_part(back, solved, h, b, 1 if b == 0 else 0, 2)
+
+    def renew_corners(h):
+        place_renewed(h, outer, [partial[h * boxes + b] - far_part(back, solved, h, b, 0 if b == 0 else 2, 1) for b in outer])
+
     def renew_far(h, bs):
-        renewed = [
-            (partial[h * boxes + b] - far_part(back, solved, h, b)).astype(jnp.bfloat16) for b in bs
-        ]
+        place_renewed(h, bs, [partial[h * boxes + b] - far_part(back, solved, h, b) for b in bs])
+
+    def place_renewed(h, bs, renewed):
+        renewed = [kept.astype(jnp.bfloat16) for kept in renewed]
         for b, kept in zip(bs, renewed):
             stacked = jnp.concatenate([kept, solved[h * window + OWN * wide + 1 + b]], axis=0)
             placed = jnp.dot(placing[b], stacked, preferred_element_type=jnp.float32).astype(jnp.bfloat16)
@@ -282,76 +307,87 @@
                     :, part * half : (part + 1) * half
                 ]
 
-    inner, outer = (1, 2), (0, last)
-
-    pl.semaphore_wait(barrier, jnp.where(has_far, 4, 3))
-
-    send_x(0, (0, last, 1, 2))
-    send_y(0)
-    send_s(0)
-    send_s(1)
-    lax.fori_loop(0, boxes, make_placing, 0)
+    loads[0].wait()
+    lax.fori_loop(0, 2, gather_outer, 0)
+    send_x(1, outer)
+    send_y(1)
+    for h in range(2):
+        send_s(h, outer)
+    lax.fori_loop(0, 2, gather_inner, 0)
+    for h in range(2):
+        send_s(h, inner)
+    loads[1].wait()
+    loads[2].wait()
+    lax.fori_loop(0, boxes, gather_redundant, 0)
+    pl.when(jnp.logical_not(has_far))(clear_far)
+    lax.fori_loop(0, boxes, find_slots, 0)
     load_coupling.wait()
     arrive_s(0)
     solve_near(0, inner)
     corner_down(0)
+    send_x(0, (1,))
     arrive_s(1)
     solve_near(1, inner)
     corner_up(0)
-    send_x(1, outer)
+    send_x(0, (2,))
+    lax.fori_loop(0, boxes, make_placing, 0)
     forward_sides(0)
-    send_y(1)
     arrive_sides(0)
+    corner_down(1)
+    send_x(1, (1,))
     solve_near(0, outer)
+    corner_up(1)
+    send_x(1, (2,))
+    forward_sides(1)
+    arrive_sides(1)
+    solve_near(1, outer)
+    load_inverse.wait()
     arrive_x(0, inner)
-    send_x(1, inner)
-    load_inverse.wait()
-    solve_far(0, inner)
-    corner_down(1)
     arrive_low_corner(0)
     arrive_high_corner(0)
     solve_far(0, outer)
-    send_s(2)
-    corner_up(1)
-    send_x(2, (0, last, 1, 2))
+    send_x(2, outer)
     send_y(2)
-    forward_sides(1)
+    send_s(2, outer)
+    solve_far(0, inner)
+    send_x(2, inner)
+    send_s(2, inner)
     load_back.wait()
     arrive_s(2)
     renew_near(0, inner)
-    arrive_sides(1)
-    solve_near(1, outer)
     arrive_x(1, inner)
-    solve_far(1, inner)
-    send_x(3, (1,))
-    corner_down(2)
     arrive_low_corner(1)
     arrive_high_corner(1)
     solve_far(1, outer)
-    send_x(3, (0, last, 2))
-    send_s(3)
+    send_x(3, outer)
+    send_y(3)
+    send_s(3, outer)
+    corner_down(2)
+    solve_far(1, inner)
+    send_x(3, inner)
+    send_s(3, inner)
     corner_up(2)
-    send_y(3)
     forward_sides(2)
     arrive_s(3)
     renew_near(1, inner)
     arrive_sides(2)
     renew_near(0, outer)
+    arrive_x(2, inner)
     corner_down(3)
-    arrive_x(2, inner)
     renew_far(0, inner)
     corner_up(3)
+    forward_sides(3)
     arrive_low_corner(2)
     arrive_high_corner(2)
     renew_far(0, outer)
-    forward_sides(3)
+    arrive_sides(3)
+    renew_near(1, outer)
     arrive_x(3, inner)
     renew_far(1, inner)
-    arrive_sides(3)
-    renew_near(1, outer)
+    renew_sides(1)
     arrive_low_corner(3)
     arrive_high_corner(3)
-    renew_far(1, outer)
+    renew_corners(1)
     for s in range(4):
         wait_sends(s)
 

time: 48.9 us -> 46.3 us (0.947)
  Pallas kernels: 47.1 us -> 44.7 us
    pallas_call x1, Pallas kernels: 47.1 us -> 44.7 us  [on_device(): pl.pallas_call(functools.partial(kernel, (rows_mesh, cols_mesh, boxes, K,...]
where the time goes in v4:
time: 46.3 us; the launch traced here: 46.2 us
  Pallas kernels  44.7 us (97%)
  local copies, waits for them, and re-layouts  1.49 us (3%)
    pallas_call x1, Pallas kernels, on_device(): pl.pallas_call(functools.partial(kernel, (rows_mesh, cols_mesh, boxes, K,...  44.7 us
    unnamed x1, local copies, waits for them, and re-layouts  1.49 us

profile of v4, /device:TPU:3, one launch (start us, length us, event | category | flops | bytes accessed | tf_op | source)
XLA Modules:
  0.0 46.2 jit_solution(17542072875849496953)
XLA Ops:
  0.0 44.7 %shard_map.73 = bf16[4,640,512]{2,1,0:T(8,128)(2,1)S(1)} custom-call(bf16[4,640,512]{2,1,0:T(8,128)(2,1)} %bitcast.15, s32[4,384]{1,0:T(4,128)} %bitcast.17, s32[4,256]{1,0:T(4,128)} %bitcast.18, s32[4,6]{1,0:T(4,128)} %bitcast.19, bf16[4,2,6,256,384]{4,3,2,1,0:T(8,128)(2,1)} %bitcast.13, bf16[4,2,6,384,256]{4,3,2,1,0:T(8,128)(2,1)} %bitcast.14, ...), custom_call_target="tpu_custom_call" | custom-call | flops 14000000000 | bytes 25000000 | tf_op jit(solution)/shard_map/pallas_call | solution.py:406
  44.7 1.5 %copy.9 = bf16[1,4,640,512]{3,2,1,0:T(8,128)(2,1)} copy(bf16[1,4,640,512]{3,2,1,0:T(8,128)(2,1)S(1)} %bitcast.12) | data formatting | bytes 5242880

commit v5 on v4

--- a/solution.py
+++ b/solution.py
@@ -374,8 +374,8 @@
     renew_near(0, outer)
     arrive_x(2, inner)
     corner_down(3)
+    corner_up(3)
     renew_far(0, inner)
-    corner_up(3)
     forward_sides(3)
     arrive_low_corner(2)
     arrive_high_corner(2)

time: 46.3 us -> 45.9 us (level)
  no operation moved by 1% of the time
where the time goes in v5:
time: 45.9 us; the launch traced here: 45.8 us
  Pallas kernels  44.3 us (97%)
  local copies, waits for them, and re-layouts  1.49 us (3%)
    pallas_call x1, Pallas kernels, on_device(): pl.pallas_call(functools.partial(kernel, (rows_mesh, cols_mesh, boxes, K,...  44.3 us
    unnamed x1, local copies, waits for them, and re-layouts  1.49 us

profile of v5, /device:TPU:3, one launch (start us, length us, event | category | flops | bytes accessed | tf_op | source)
XLA Modules:
  0.0 45.8 jit_solution(8730029250204533183)
XLA Ops:
  0.0 44.3 %shard_map.73 = bf16[4,640,512]{2,1,0:T(8,128)(2,1)S(1)} custom-call(bf16[4,640,512]{2,1,0:T(8,128)(2,1)} %bitcast.15, s32[4,384]{1,0:T(4,128)} %bitcast.17, s32[4,256]{1,0:T(4,128)} %bitcast.18, s32[4,6]{1,0:T(4,128)} %bitcast.19, bf16[4,2,6,256,384]{4,3,2,1,0:T(8,128)(2,1)} %bitcast.13, bf16[4,2,6,384,256]{4,3,2,1,0:T(8,128)(2,1)} %bitcast.14, ...), custom_call_target="tpu_custom_call" | custom-call | flops 14000000000 | bytes 25000000 | tf_op jit(solution)/shard_map/pallas_call | solution.py:406
  44.3 1.5 %copy.9 = bf16[1,4,640,512]{3,2,1,0:T(8,128)(2,1)} copy(bf16[1,4,640,512]{3,2,1,0:T(8,128)(2,1)S(1)} %bitcast.12) | data formatting | bytes 5242880
